TPU v7x, 512 devices: a whole 4x4x16 slice. The times are simulated.
512 devices in a mesh: layer: 64 (over x, y, z_hi, core), tok: 8 (over z_lo).
Axes of the slice: x: 4, y: 4, z: 16 (z_hi: 2, z_lo: 8; z = z_hi * 8 + z_lo), core: 2. Of those that a mesh axis runs over, the one named last changes fastest.
Arguments:
- residuals: bfloat16 [2, 512, 8192], P(None, None, 'layer'), may hold values from -6 to 6
- w_enc: bfloat16 [2, 8192, 16384], P(None, 'layer', 'tok'), may hold values from -0.0625 to 0.0625
- b_enc: float32 [2, 16384], P(None, 'tok'), may hold values from -3 to 3
- w_dec: bfloat16 [2, 16384, 16384], P(None, 'tok', 'layer'), may hold values from -0.0625 to 0.0625
- b_dec: float32 [16384], P('layer'), may hold values from -3 to 3
- act_slots: int32 [2, 8, 32], replicated, may hold values from -1 to 127, as said below
Outputs:
- recon: bfloat16 [512, 16384], P('tok', 'layer')
Inputs may be any that keep to these rules, and one draw needn't show every extreme that they name: `act_slots`: entry k of a list names a block among the 16 blocks numbered from (k // 4) * 16, or is -1 for an empty slot. In each group of 4 slots the live entries come first and at least one is live; blocks within a list are distinct; in every list some group is full.
All inputs are finite; a program needn't handle non-finite values.
Results may differ from a plain program's by a relative error of at most 0.0043.
Values may be sent and summed in bfloat16 or wider, within the bound.
A program may use at most 64 MiB of HBM per device.

v0:
```python
import jax
import jax.numpy as jnp
from jax import lax
from jax.sharding import PartitionSpec as P


def per_device(residuals, w_enc, b_enc, w_dec, b_dec, act_slots):
    tok_count = lax.axis_size("tok")
    tok_index = lax.axis_index("tok")
    sources, tokens, d_local = residuals.shape
    blocks = w_enc.shape[2] // 128
    columns = w_dec.shape[2]
    block_lists = act_slots.shape[1]
    slot_width = act_slots.shape[2] // tok_count
    block_rows = tokens // block_lists
    packed = slot_width * 128
    own_slots = lax.dynamic_slice_in_dim(act_slots, tok_index * slot_width, slot_width, 2)
    is_live = own_slots >= 0
    local_ids = jnp.where(is_live, own_slots - tok_index * blocks, 0)
    keep_mask = jnp.repeat(is_live.astype(jnp.float32), 128, axis=2)
    enc_blocks = w_enc.reshape(sources, d_local, blocks, 128)
    bias_blocks = b_enc.reshape(sources, blocks, 128)
    dec_blocks = w_dec.reshape(sources, blocks, 128, columns)
    x_blocks = residuals.reshape(sources, block_lists, block_rows, d_local)
    pre_list = []
    bias_list = []
    for source in range(sources):
        chosen = jnp.take(enc_blocks[source], local_ids[source], axis=1)
        pre_part = jnp.einsum(
            "btd,dbcf->btcf", x_blocks[source], chosen, preferred_element_type=jnp.float32
        )
        pre_list.append(pre_part.reshape(block_lists * block_rows, packed))
        bias_list.append(
            jnp.take(bias_blocks[source], local_ids[source], axis=0).reshape(block_lists, packed)
        )
    pre_part = jnp.stack(pre_list)
    bias_sel = jnp.stack(bias_list)
    summed = lax.psum(pre_part, "layer").reshape(sources, block_lists, block_rows, packed)
    active = jnp.maximum(summed + bias_sel[:, :, None, :], 0.0) * keep_mask[:, :, None, :]
    features = active.astype(jnp.bfloat16).reshape(sources, tokens, packed)
    feature_blocks = features.reshape(sources, block_lists, block_rows, packed)
    partials = jnp.zeros((block_lists, block_rows, columns), jnp.float32)
    for source in range(sources):
        decoder = jnp.take(dec_blocks[source], local_ids[source], axis=0).reshape(
            block_lists, packed, columns
        )
        partials = partials + jnp.einsum(
            "btk,bkc->btc", feature_blocks[source], decoder, preferred_element_type=jnp.float32
        )
    partials = partials.reshape(tokens, columns)
    owned = lax.psum_scatter(partials, "tok", scatter_dimension=0, tiled=True)
    return (owned + b_dec[None, :]).astype(jnp.bfloat16)


def solution(mesh):
    in_specs = (
        P(None, None, "layer"),
        P(None, "layer", "tok"),
        P(None, "tok"),
        P(None, "tok", "layer"),
        P("layer"),
        P(),
    )
    out_specs = P("tok", "layer")
    return jax.shard_map(
        per_device, mesh=mesh, in_specs=in_specs, out_specs=out_specs, check_vma=False
    )
```

profile of v0, /device:TPU:7, one launch (start us, length us, event | category | flops | bytes accessed | tf_op | source)
XLA Modules:
  0.0 1178.8 jit_solution(14819480103277169398)
XLA Ops:
  6.5 0.8 fusion.11
  7.3 0.8 subtract_select_fusion
  8.1 0.1 copy.47
  8.2 0.1 copy.41
  8.3 0.1 copy.48
  8.4 0.1 copy.42
  8.5 0.1 copy.44
  8.6 0.1 reshape.114
  8.6 0.1 copy.50
  8.7 0.1 reshape.118
  8.8 1.0 fusion.14
  9.8 1.3 fusion.13
  11.1 0.3 copy.64
  11.4 0.3 copy.45
  11.7 0.8 gather_fusion
  12.4 0.4 convolution_bitcast_fusion.1
  12.8 0.7 copy.46
  13.5 0.4 stack_reshape.12
  13.9 0.3 copy.65
  14.2 0.3 copy.51
  14.5 0.8 gather_fusion.1
  15.3 0.4 convolution_bitcast_fusion
  15.7 0.7 copy.52
  16.4 0.4 stack_reshape.13
  16.8 1.5 pad_maximum_fusion
  18.3 0.0 all-reduce.2.cloned.1.call-update
  18.3 0.0 reduce-scatter.2.cloned.1.call-start
  18.4 0.6 copy-done.2
  19.0 0.1 copy.57
  19.1 0.6 gather_fusion.3
  19.7 0.1 broadcast_select_fusion.2
  19.8 0.6 gather_fusion.2
  20.3 0.1 broadcast_select_fusion.3
  20.4 1.7 fusion.12
  22.1 2.0 gather_fusion.4
  24.1 2.0 gather_fusion.5
  26.2 0.1 broadcast_bitcast_fusion
  26.2 2.0 broadcast_select_fusion.1
  28.2 0.2 copy-done.1
  28.5 1.6 broadcast_select_fusion
  30.0 1042.1 %all-reduce.2.cloned.1.call-done = f32[2,8,64,512]{3,2,1,0:T(8,128)} async-done(((f32[2,8,64,512]{3,2,1,0:T(8,128)}), f32[2,8,64,512]{3,2,1,0:T(8,128)}) %all-reduce.2.cloned.1.call-update) | async-done | bytes 2097168 | tf_op jit(solution)/shard_map/psum | solution.py:38
  1072.1 1.9 multiply_convert_fusion
  1074.1 0.5 fusion.6
  1074.6 1.1 copy-done
  1075.7 1.3 convolution_add_fusion
  1076.9 0.0 reduce-scatter.2.cloned.1.call-update
  1077.0 93.5 %reduce-scatter.2.cloned.1.call-done = f32[64,256]{1,0:T(8,128)} async-done(((f32[512,256]{1,0:T(8,128)}), f32[64,256]{1,0:T(8,128)}) %reduce-scatter.2.cloned.1.call-update) | async-done | bytes 65552 | tf_op jit(solution)/shard_map/reduce_scatter | solution.py:51
  1170.5 1.5 add_convert_fusion
  (17 shorter events, 0.1 us)
Async XLA Ops:
  6.5 1065.6 %all-reduce.2.cloned.1.call-start = ((), (), s32[]{:S(2)}) async-start(), calls=%async_computation.1 | async-start | bytes 4194304 | tf_op jit(solution)/shard_map/psum | solution.py:38
  18.3 0.7 copy-start.2
  18.3 1152.2 %reduce-scatter.2.cloned.1.call-start = ((), (), s32[]{:S(2)}) async-start(), calls=%async_computation.2 | async-start | bytes 589824 | tf_op jit(solution)/shard_map/reduce_scatter | solution.py:51
  26.2 2.2 copy-start.1
  1074.1 1.6 copy-start
  1075.7 94.8 %copy-start.3 = (f32[256]{0:T(256)S(1)}, f32[256]{0:T(256)}, u32[]{:S(2)}) copy-start(f32[256]{0:T(256)} %param.16) | copy-start | bytes 3076
Sparse Core Ops, SparseCore 0:
  18.4 1053.6 all-reduce.1
  1077.1 93.3 reduce-scatter.1
where the time goes:
time: 1180 us
  waiting for transfers between devices  1140 us (97%)
  local copies, waits for them, and re-layouts  16.8 us (1%)
  between operations  13.6 us (1%)
    psum x1, waiting for transfers between devices, per_device(): lax.psum(pre_part, 'layer')  1040 us
    reduce_scatter x1, waiting for transfers between devices, per_device(): owned = lax.psum_scatter(partials, 'tok', scatter_dimension=0, tiled=True)  93.5 us
  transfers between devices with their start and end apart: 2, of which 2 were waited for; matrix products, arithmetic and copies ran while one was open for 1% of the time, Pallas kernels for 0%

commit v1 on v0

v1 whole, which is shorter than its diff:
```python
import functools

import jax
import jax.numpy as jnp
from jax import lax
from jax.experimental import pallas as pl
from jax.experimental.pallas import tpu as pltpu
from jax.sharding import PartitionSpec as P

MESH = pl.DeviceIdType.MESH
CHUNKS = 2
F32 = jnp.float32
BF16 = jnp.bfloat16


def device(x, y, zh, c, t):
    return (((x * 4 + y) * 2 + zh) * 2 + c, t)


def kernel(
    slots_ref, x_hbm, we_hbm, be_hbm, wd_hbm, out_ref,
    xfull, wfull, be, wd, pbuf, rs_land, zh_send, zh_land, fown, feat, zbuf, zland,
    local_sem, in_send, in_recv, wd_send, wd_recv, rs_send, rs_recv, zh_ss, zh_rs,
    ag_send, own_send, ag_recv, zl_send, zl_recv,
):
    layer = lax.axis_index("layer")
    t = lax.axis_index("tok")
    c = lax.rem(layer, 2)
    zh = lax.rem(layer // 2, 2)
    y = lax.rem(layer // 4, 4)
    x = layer // 16
    p = x * 4 + y
    half = lax.rem(p // 4, 2)
    pair = p // 8
    partner = device(x, y, zh, 1 - c, t)
    opposite = device(x, y, 1 - zh, c, t)

    def plane(d):
        return lax.rem(x + d // 4, 4), lax.rem(y + lax.rem(d, 4), 4)

    barrier = pltpu.get_barrier_semaphore()

    def signal(dev):
        pl.semaphore_signal(barrier, inc=1, device_id=dev, device_id_type=MESH)

    signal(partner)
    signal(opposite)

    def greet_plane(d, carry):
        px, py = plane(d)
        signal(device(px, py, zh, 0, t))
        signal(device(px, py, zh, 1, t))
        return carry

    def greet_line(d, carry):
        pt = lax.rem(t + d, 8)
        signal(device(x, y, zh, 0, pt))
        signal(device(x, y, zh, 1, pt))
        return carry

    lax.fori_loop(1, 16, greet_plane, 0)
    lax.fori_loop(1, 8, greet_line, 0)

    local = [
        pltpu.make_async_copy(x_hbm.at[c], xfull.at[:, pl.ds(0, 128)], local_sem.at[1]),
        pltpu.make_async_copy(wd_hbm, wd.at[0], local_sem.at[3]),
    ]
    for i in range(16):
        part = pl.ds(i * 128, 128)
        pltpu.make_async_copy(we_hbm.at[c, :, part], wfull.at[i, pl.ds(0, 128)], local_sem.at[0]).start()
    for copy in local:
        copy.start()
    for i in range(16):
        pltpu.make_async_copy(be_hbm.at[:, pl.ds(i * 128, 128)], be.at[i], local_sem.at[2]).start()

    pl.semaphore_wait(barrier, 2 + 30 + 14)

    def remote(src, dst, send, recv, dev):
        return pltpu.make_async_remote_copy(
            src_ref=src, dst_ref=dst, send_sem=send, recv_sem=recv, device_id=dev, device_id_type=MESH
        )

    swap_w = [
        remote(
            we_hbm.at[1 - c, :, pl.ds(i * 128, 128)], wfull.at[i, pl.ds(128, 128)],
            in_send.at[0], in_recv.at[0], partner,
        )
        for i in range(16)
    ]
    half_w = wfull.at[:, pl.ds(128, 128)]
    swap_x = remote(x_hbm.at[1 - c], xfull.at[:, pl.ds(128, 128)], in_send.at[1], in_recv.at[1], partner)
    swap_d = remote(wd_hbm, wd.at[1], wd_send, wd_recv, partner)
    for copy in swap_w:
        copy.start()
    swap_x.start()
    pltpu.make_async_copy(half_w, half_w, local_sem.at[0]).wait()
    local[0].wait()
    pltpu.make_async_copy(half_w, half_w, in_recv.at[0]).wait()
    swap_x.wait_recv()
    swap_d.start()

    def block_id(source, b, s):
        slot = slots_ref[source, b, 4 * t + s]
        return jnp.maximum(slot - 16 * t, 0), jnp.minimum(slot + 1, 1)

    for k in range(CHUNKS):
        for j in range(4):
            b = 4 * k + j
            cols = [wfull[block_id(c, b, s)[0]] for s in range(4)]
            w = jnp.concatenate(cols, axis=1)
            part = jnp.dot(xfull[pl.ds(b * 64, 64), :], w, preferred_element_type=F32)
            pbuf[k, pl.ds(j * 64, 64), :] = part.astype(BF16)

        def send_part(d, carry, k=k):
            px, py = plane(d)
            q = px * 4 + py
            remote(
                pbuf.at[k, pl.ds(pl.multiple_of(q * 16, 16), 16)], rs_land.at[k, d - 1],
                rs_send.at[k], rs_recv.at[k], device(px, py, zh, c, t),
            ).start()
            return carry

        lax.fori_loop(1, 16, send_part, 0)

    sums = []
    for k in range(CHUNKS):
        pltpu.make_async_copy(rs_land.at[k], rs_land.at[k], rs_recv.at[k]).wait()
        total = pbuf[k, pl.ds(pl.multiple_of(p * 16, 16), 16), :].astype(F32)
        for d in range(15):
            total = total + rs_land[k, d].astype(F32)
        sums.append(total)
        zh_send[k] = total.astype(BF16)
        remote(zh_send.at[k], zh_land.at[k], zh_ss.at[k], zh_rs.at[k], opposite).start()

    pltpu.make_async_copy(be, be, local_sem.at[2]).wait()
    rows = pl.ds(pl.multiple_of(lax.rem(p, 4) * 16, 16), 16)
    for k in range(CHUNKS):
        b = 4 * k + p // 4
        biases, masks = [], []
        for s in range(4):
            i, live = block_id(c, b, s)
            both = be[i]
            biases.append(jnp.where(c == 0, both[0:1], both[1:2]))
            masks.append(jnp.full((1, 128), live.astype(F32)))
        bias = jnp.concatenate(biases, axis=1)
        mask = jnp.concatenate(masks, axis=1)
        remote(zh_send.at[k], zh_land.at[k], zh_ss.at[k], zh_rs.at[k], opposite).wait_recv()
        pre = sums[k] + zh_land[k].astype(F32) + bias
        fown[k] = (jnp.maximum(pre, 0.0) * mask).astype(BF16)
        mine = feat.at[k, pair, c, rows]

        def send_features(d, carry, k=k, mine=mine):
            px, py = plane(d)
            remote(fown.at[k], mine, ag_send.at[k], ag_recv.at[k, pair], device(px, py, zh, half, t)).start()
            return carry

        @pl.when(c == half)
        def _(k=k, mine=mine):
            pltpu.make_async_copy(fown.at[k], mine, ag_recv.at[k, pair]).start()

        @pl.when(c != half)
        def _(k=k, mine=mine):
            remote(fown.at[k], mine, own_send.at[k], ag_recv.at[k, pair], partner).start()

        lax.fori_loop(1, 16, send_features, 0)

    local[1].wait()
    swap_d.wait_recv()
    for k in range(CHUNKS):
        for j in range(2):
            m = 2 * k + j
            b = 2 * m + c
            pltpu.make_async_copy(feat.at[k, j], feat.at[k, j], ag_recv.at[k, j]).wait()
            ids = [[block_id(s, b, i)[0] for i in range(4)] for s in range(2)]
            f = jnp.concatenate([feat[k, j, 0], feat[k, j, 1]], axis=1)
            for side in range(2):
                w = jnp.concatenate(
                    [
                        wd[side, s, ids[s][i]]
                        for s in range(2)
                        for i in range(4)
                    ],
                    axis=0,
                )
                zbuf[m, side] = jnp.dot(f, w, preferred_element_type=F32).astype(BF16)

            for side in range(2):
                core = c if side == 0 else 1 - c
                whole = remote(
                    zbuf.at[m, side], zland.at[t], zl_send.at[m, side], zl_recv, device(x, y, zh, core, b)
                )
                if side == 0:

                    @pl.when(b == t)
                    def _(m=m):
                        pltpu.make_async_copy(zbuf.at[m, 0], zland.at[t], zl_recv).start()

                    @pl.when(b != t)
                    def _(whole=whole):
                        whole.start()
                else:
                    whole.start()

    pltpu.make_async_copy(zland, zland, zl_recv).wait()
    result = zland[0].astype(F32)
    for i in range(1, 8):
        result = result + zland[i].astype(F32)
    out_ref[...] = result

    pltpu.make_async_copy(half_w, half_w, in_send.at[0]).wait()
    swap_x.wait_send()
    swap_d.wait_send()
    for k in range(CHUNKS):
        pltpu.make_async_copy(rs_land.at[k], rs_land.at[k], rs_send.at[k]).wait()
        pltpu.make_async_copy(rs_land.at[k], rs_land.at[k], ag_send.at[k]).wait()
        remote(zh_send.at[k], zh_land.at[k], zh_ss.at[k], zh_rs.at[k], opposite).wait_send()

        @pl.when(c != half)
        def _(k=k):
            remote(fown.at[k], fown.at[k], own_send.at[k], ag_recv.at[k, pair], partner).wait_send()

    for m in range(4):
        b = 2 * m + c

        @pl.when(b != t)
        def _(m=m):
            remote(zbuf.at[m, 0], zland.at[t], zl_send.at[m, 0], zl_recv, partner).wait_send()

        remote(zbuf.at[m, 1], zland.at[t], zl_send.at[m, 1], zl_recv, partner).wait_send()


def per_device(residuals, w_enc, b_enc, w_dec, b_dec, act_slots):
    dma = pltpu.SemaphoreType.DMA
    summed = pl.pallas_call(
        kernel,
        out_shape=jax.ShapeDtypeStruct((64, 256), F32),
        in_specs=[pl.BlockSpec(memory_space=pltpu.SMEM)] + [pl.BlockSpec(memory_space=pl.ANY)] * 4,
        out_specs=pl.BlockSpec(memory_space=pltpu.VMEM),
        scratch_shapes=[
            pltpu.VMEM((512, 256), BF16),
            pltpu.VMEM((16, 256, 128), BF16),
            pltpu.VMEM((16, 2, 128), F32),
            pltpu.VMEM((2, 2, 16, 128, 256), BF16),
            pltpu.VMEM((CHUNKS, 256, 512), BF16),
            pltpu.VMEM((CHUNKS, 15, 16, 512), BF16),
            pltpu.VMEM((CHUNKS, 16, 512), BF16),
            pltpu.VMEM((CHUNKS, 16, 512), BF16),
            pltpu.VMEM((CHUNKS, 16, 512), BF16),
            pltpu.VMEM((CHUNKS, 2, 2, 64, 512), BF16),
            pltpu.VMEM((4, 2, 64, 256), BF16),
            pltpu.VMEM((8, 64, 256), BF16),
            dma((4,)),
            dma((2,)),
            dma((2,)),
            dma,
            dma,
            dma((CHUNKS,)),
            dma((CHUNKS,)),
            dma((CHUNKS,)),
            dma((CHUNKS,)),
            dma((CHUNKS,)),
            dma((CHUNKS,)),
            dma((CHUNKS, 2)),
            dma((4, 2)),
            dma,
        ],
        compiler_params=pltpu.CompilerParams(
            collective_id=0, has_side_effects=True, vmem_limit_bytes=60 * 2**20
        ),
        cost_estimate=pl.CostEstimate(flops=402653184, bytes_accessed=4194304, transcendentals=0),
    )(act_slots, residuals, w_enc, b_enc, w_dec.reshape(2, 16, 128, 256))
    return (summed + b_dec[None, :]).astype(BF16)


def solution(mesh):
    in_specs = (
        P(None, None, "layer"),
        P(None, "layer", "tok"),
        P(None, "tok"),
        P(None, "tok", "layer"),
        P("layer"),
        P(),
    )
    return jax.shard_map(
        per_device, mesh=mesh, in_specs=in_specs, out_specs=P("tok", "layer"), check_vma=False
    )
```

time: 1180 us -> 53.6 us (0.05)
  waiting for transfers between devices: 1140 us -> 0 us
  Pallas kernels: 0 us -> 51.9 us
  local copies, waits for them, and re-layouts: 16.8 us -> 0.01 us
  between operations: 13.6 us -> 0.02 us
    psum x1 -> x0, waiting for transfers between devices: 1040 us -> none  [per_device(): lax.psum(pre_part, 'layer')]
    reduce_scatter x1 -> x0, waiting for transfers between devices: 93.5 us -> none  [per_device(): owned = lax.psum_scatter(partials, 'tok', scatter_dimension=0, tiled=True)]
    pallas_call x0 -> x1, Pallas kernels: none -> 51.9 us  [per_device(): pl.pallas_call(kernel, out_shape=jax.ShapeDtypeStruct((64, 256), F32), in...]
  transfers between devices with their start and end apart: 2 -> 0, of which waited for: 2 -> 0; matrix products, arithmetic and copies ran while one was open for 1% -> 0% of each run, Pallas kernels for 0% -> 0%
where the time goes in v1:
time: 53.6 us; the launch traced here: 53.4 us
  Pallas kernels  51.9 us (97%)
  other arithmetic  1.46 us (3%)
    pallas_call x1, Pallas kernels, per_device(): pl.pallas_call(kernel, out_shape=jax.ShapeDtypeStruct((64, 256), F32), in...  51.9 us
    convert_element_type x1, other arithmetic, per_device(): return (summed + b_dec[None, :]).astype(BF16)  1.46 us

profile of v1, /device:TPU:7, one launch (start us, length us, event | category | flops | bytes accessed | tf_op | source)
XLA Modules:
  0.0 53.4 jit_solution(14874576427174727374)
XLA Ops:
  0.0 0.0 copy-start
  0.0 51.9 %shard_map.64 = f32[64,256]{1,0:T(8,128)} custom-call(s32[2,8,32]{2,1,0:T(8,128)} %slots_ref.1, bf16[2,512,128]{2,1,0:T(8,128)(2,1)} %x_hbm.1, bf16[2,128,2048]{2,1,0:T(8,128)(2,1)} %we_hbm.1, f32[2,2048]{1,0:T(2,128)} %be_hbm.1, bf16[2,16,128,256]{3,2,1,0:T(8,128)(2,1)} %bitcast.1), custom_call_target="tpu_custom_call" | custom-call | flops 402653184 | bytes 4194304 | tf_op jit(solution)/shard_map/pallas_call | solution.py:234
  51.9 0.0 copy-done
  51.9 1.5 %add_convert_fusion = bf16[64,256]{1,0:T(8,128)(2,1)} fusion(f32[64,256]{1,0:T(8,128)} %shard_map.64, f32[256]{0:T(256)S(1)} %copy-done), kind=kLoop, calls=%fused_computation | loop fusion | flops 32768 | bytes 99328 | tf_op jit(solution)/shard_map/convert_element_type | solution.py:272
Async XLA Ops:
  0.0 51.9 %copy-start = (f32[256]{0:T(256)S(1)}, f32[256]{0:T(256)}, u32[]{:S(2)}) copy-start(f32[256]{0:T(256)} %param.10) | copy-start | bytes 3076

commit v2 on v1

v2 whole, which is shorter than its diff:
```python
import functools

import jax
import jax.numpy as jnp
from jax import lax
from jax.experimental import pallas as pl
from jax.experimental.pallas import tpu as pltpu
from jax.sharding import PartitionSpec as P

MESH = pl.DeviceIdType.MESH
CHUNKS = 2
F32 = jnp.float32
BF16 = jnp.bfloat16


def device(x, y, zh, c, t):
    return (((x * 4 + y) * 2 + zh) * 2 + c, t)


def kernel(
    slots_ref, x_hbm, we_hbm, be_hbm, wd_hbm, bd_ref, out_ref,
    xv, we, be, wd, keep, give, take, pbuf, rs_land, zh_send, zh_land, fown, feat, zbuf, zland,
    local_sem, give_send, give_recv, wd_send, wd_recv, rs_send, rs_recv, zh_ready, zh_ss, zh_rs,
    ag_send, own_send, ag_recv, zl_send, zl_recv,
):
    layer = lax.axis_index("layer")
    t = lax.axis_index("tok")
    c = lax.rem(layer, 2)
    zh = lax.rem(layer // 2, 2)
    y = lax.rem(layer // 4, 4)
    x = layer // 16
    p = x * 4 + y
    half = lax.rem(x, 2)
    pair = x // 2
    crossed = lax.rem(half + c, 2)
    partner = device(x, y, zh, 1 - c, t)
    opposite = device(x, y, 1 - zh, c, t)

    def plane(d):
        return lax.rem(x + d // 4, 4), lax.rem(y + lax.rem(d, 4), 4)

    barrier = pltpu.get_barrier_semaphore()

    def signal(dev):
        pl.semaphore_signal(barrier, inc=1, device_id=dev, device_id_type=MESH)

    def greet_same(d, carry):
        px, py = plane(d)
        signal(device(px, py, zh, c, t))
        return carry

    def greet_other(d, carry):
        px, py = c + 2 * (d // 4), lax.rem(d, 4)

        @pl.when((px != x) | (py != y))
        def _():
            signal(device(px, py, zh, 1 - c, t))

        return carry

    def greet_line(d, carry):
        signal(device(x, y, zh, lax.rem(t, 2), lax.rem(t + d, 8)))
        return carry

    lax.fori_loop(1, 16, greet_same, 0)
    lax.fori_loop(0, 8, greet_other, 0)
    signal(partner)
    lax.fori_loop(1, 8, greet_line, 0)

    @pl.when(zh == 0)
    def _():
        signal(opposite)

    load_x = pltpu.make_async_copy(x_hbm, xv, local_sem.at[0])
    load_d = pltpu.make_async_copy(wd_hbm, wd.at[0], local_sem.at[3])
    load_x.start()
    for s in range(2):
        for i in range(16):
            cut = pl.ds(i * 128, 128)
            pltpu.make_async_copy(we_hbm.at[s, :, cut], we.at[s, i], local_sem.at[1]).start()
    load_d.start()
    for i in range(16):
        pltpu.make_async_copy(be_hbm.at[:, pl.ds(i * 128, 128)], be.at[i], local_sem.at[2]).start()
    load_x.wait()
    pltpu.make_async_copy(we, we, local_sem.at[1]).wait()

    def remote(src, dst, send, recv, dev):
        return pltpu.make_async_remote_copy(
            src_ref=src, dst_ref=dst, send_sem=send, recv_sem=recv, device_id=dev, device_id_type=MESH
        )

    def block_id(source, b, s):
        slot = slots_ref[source, b, 4 * t + s]
        return jnp.maximum(slot - 16 * t, 0), jnp.minimum(slot + 1, 1)

    for target, source in ((keep, c), (give, 1 - c)):
        for b in range(8):
            w = jnp.concatenate([we[source, block_id(source, b, s)[0]] for s in range(4)], axis=1)
            target[b] = jnp.dot(xv[source, pl.ds(b * 64, 64), :], w, preferred_element_type=F32)

    pl.semaphore_wait(barrier, 15 + 15 * crossed + 1 + 6 + 2 * lax.rem(t + c, 2) + zh)

    @pl.when(zh == 1)
    def _():
        pl.semaphore_signal(zh_ready, inc=1, device_id=opposite, device_id_type=MESH)

    gives = []
    for k in range(CHUNKS):
        for i in range(4):
            n = 4 * k + lax.rem(x + i, 4)
            gives.append(remote(give.at[n], take.at[n], give_send.at[k, i], give_recv.at[k, i], partner))
            gives[-1].start()
    for k in range(CHUNKS):
        for i in range(4):
            px = lax.rem(x + i, 4)
            n = 4 * k + px
            gives[4 * k + i].wait_recv()
            pbuf[n] = (keep[n] + take[n]).astype(BF16)

            def send_part(j, carry, k=k, i=i, px=px, n=n):
                py = lax.rem(y + j, 4)
                remote(
                    pbuf.at[n, pl.ds(pl.multiple_of(py * 16, 16), 16)], rs_land.at[k, 4 * i + j - 1],
                    rs_send.at[k], rs_recv.at[k], device(px, py, zh, c, t),
                ).start()
                return carry

            lax.fori_loop(1 if i == 0 else 0, 4, send_part, 0)

    swap_d = remote(wd_hbm, wd.at[1], wd_send, wd_recv, partner)
    swap_d.start()

    @pl.when(zh == 0)
    def _():
        pl.semaphore_wait(zh_ready, 1)

    rows = pl.ds(pl.multiple_of(y * 16, 16), 16)
    sums = []
    for k in range(CHUNKS):
        pltpu.make_async_copy(rs_land.at[k], rs_land.at[k], rs_recv.at[k]).wait()
        total = pbuf[4 * k + x, rows, :].astype(F32)
        for d in range(15):
            total = total + rs_land[k, d].astype(F32)
        sums.append(total)
        zh_send[k] = total.astype(BF16)
        remote(zh_send.at[k], zh_land.at[k], zh_ss.at[k], zh_rs.at[k], opposite).start()

    pltpu.make_async_copy(be, be, local_sem.at[2]).wait()
    for k in range(CHUNKS):
        b = 4 * k + x
        biases, masks = [], []
        for s in range(4):
            i, live = block_id(c, b, s)
            both = be[i]
            biases.append(jnp.where(c == 0, both[0:1], both[1:2]))
            masks.append(jnp.full((1, 128), live.astype(F32)))
        bias = jnp.concatenate(biases, axis=1)
        mask = jnp.concatenate(masks, axis=1)
        remote(zh_send.at[k], zh_land.at[k], zh_ss.at[k], zh_rs.at[k], opposite).wait_recv()
        pre = sums[k] + zh_land[k].astype(F32) + bias
        fown[k] = (jnp.maximum(pre, 0.0) * mask).astype(BF16)
        mine = feat.at[k, pair, c, rows]

        def send_features(d, carry, k=k, mine=mine):
            px, py = plane(d)
            remote(fown.at[k], mine, ag_send.at[k], ag_recv.at[k, pair], device(px, py, zh, half, t)).start()
            return carry

        lax.fori_loop(1, 16, send_features, 0)

        @pl.when(c == half)
        def _(k=k, mine=mine):
            pltpu.make_async_copy(fown.at[k], mine, ag_recv.at[k, pair]).start()

        @pl.when(c != half)
        def _(k=k, mine=mine):
            remote(fown.at[k], mine, own_send.at[k], ag_recv.at[k, pair], partner).start()

    load_d.wait()
    swap_d.wait_recv()
    for k in range(CHUNKS):
        for j in range(2):
            m = 2 * k + j
            b = 2 * m + c
            pltpu.make_async_copy(feat.at[k, j], feat.at[k, j], ag_recv.at[k, j]).wait()
            ids = [[block_id(s, b, i)[0] for i in range(4)] for s in range(2)]
            f = jnp.concatenate([feat[k, j, 0], feat[k, j, 1]], axis=1)

            for side in range(2):
                w = jnp.concatenate([wd[side, s, ids[s][i]] for s in range(2) for i in range(4)], axis=0)
                zbuf[m, side] = jnp.dot(f, w, preferred_element_type=F32).astype(BF16)
                core = c if side == 0 else 1 - c
                whole = remote(
                    zbuf.at[m, side], zland.at[t], zl_send.at[m, side], zl_recv, device(x, y, zh, core, b)
                )
                if side == 0:

                    @pl.when(b == t)
                    def _(m=m):
                        pltpu.make_async_copy(zbuf.at[m, 0], zland.at[t], zl_recv).start()

                    @pl.when(b != t)
                    def _(whole=whole):
                        whole.start()
                else:
                    whole.start()

    pltpu.make_async_copy(zland, zland, zl_recv).wait()
    result = zland[0].astype(F32)
    for i in range(1, 8):
        result = result + zland[i].astype(F32)
    out_ref[...] = (result + bd_ref[...]).astype(BF16)

    swap_d.wait_send()
    for copy in gives:
        copy.wait_send()
    for k in range(CHUNKS):
        pltpu.make_async_copy(rs_land.at[k], rs_land.at[k], rs_send.at[k]).wait()
        pltpu.make_async_copy(rs_land.at[k], rs_land.at[k], ag_send.at[k]).wait()
        remote(zh_send.at[k], zh_land.at[k], zh_ss.at[k], zh_rs.at[k], opposite).wait_send()

        @pl.when(c != half)
        def _(k=k):
            remote(fown.at[k], fown.at[k], own_send.at[k], ag_recv.at[k, pair], partner).wait_send()

    for m in range(4):
        b = 2 * m + c

        @pl.when(b != t)
        def _(m=m):
            remote(zbuf.at[m, 0], zland.at[t], zl_send.at[m, 0], zl_recv, partner).wait_send()

        remote(zbuf.at[m, 1], zland.at[t], zl_send.at[m, 1], zl_recv, partner).wait_send()


def per_device(residuals, w_enc, b_enc, w_dec, b_dec, act_slots):
    dma = pltpu.SemaphoreType.DMA
    return pl.pallas_call(
        kernel,
        out_shape=jax.ShapeDtypeStruct((64, 256), BF16),
        in_specs=[pl.BlockSpec(memory_space=pltpu.SMEM)]
        + [pl.BlockSpec(memory_space=pl.ANY)] * 4
        + [pl.BlockSpec(memory_space=pltpu.VMEM)],
        out_specs=pl.BlockSpec(memory_space=pltpu.VMEM),
        scratch_shapes=[
            pltpu.VMEM((2, 512, 128), BF16),
            pltpu.VMEM((2, 16, 128, 128), BF16),
            pltpu.VMEM((16, 2, 128), F32),
            pltpu.VMEM((2, 2, 16, 128, 256), BF16),
            pltpu.VMEM((8, 64, 512), F32),
            pltpu.VMEM((8, 64, 512), F32),
            pltpu.VMEM((8, 64, 512), F32),
            pltpu.VMEM((8, 64, 512), BF16),
            pltpu.VMEM((CHUNKS, 15, 16, 512), BF16),
            pltpu.VMEM((CHUNKS, 16, 512), BF16),
            pltpu.VMEM((CHUNKS, 16, 512), BF16),
            pltpu.VMEM((CHUNKS, 16, 512), BF16),
            pltpu.VMEM((CHUNKS, 2, 2, 64, 512), BF16),
            pltpu.VMEM((4, 2, 64, 256), BF16),
            pltpu.VMEM((8, 64, 256), BF16),
            dma((4,)),
            dma((CHUNKS, 4)),
            dma((CHUNKS, 4)),
            dma,
            dma,
            dma((CHUNKS,)),
            dma((CHUNKS,)),
            pltpu.SemaphoreType.REGULAR,
            dma((CHUNKS,)),
            dma((CHUNKS,)),
            dma((CHUNKS,)),
            dma((CHUNKS,)),
            dma((CHUNKS, 2)),
            dma((4, 2)),
            dma,
        ],
        compiler_params=pltpu.CompilerParams(
            collective_id=0, has_side_effects=True, vmem_limit_bytes=60 * 2**20
        ),
        cost_estimate=pl.CostEstimate(flops=402653184, bytes_accessed=4194304, transcendentals=0),
    )(act_slots, residuals, w_enc, b_enc, w_dec.reshape(2, 16, 128, 256), b_dec.reshape(1, 256))


def solution(mesh):
    in_specs = (
        P(None, None, "layer"),
        P(None, "layer", "tok"),
        P(None, "tok"),
        P(None, "tok", "layer"),
        P("layer"),
        P(),
    )
    return jax.shard_map(
        per_device, mesh=mesh, in_specs=in_specs, out_specs=P("tok", "layer"), check_vma=False
    )
```

time: 53.6 us -> 51.9 us (0.968)
  Pallas kernels: 51.9 us -> 50.3 us
  other arithmetic: 1.46 us -> 0 us
  local copies, waits for them, and re-layouts: 0.01 us -> 1.38 us
    pallas_call x1, Pallas kernels: 51.9 us -> 50.3 us  [per_device(): pl.pallas_call(kernel, out_shape=jax.ShapeDtypeStruct((64, 256), BF16), i...]
    convert_element_type x1 -> x0, other arithmetic: 1.46 us -> none  [per_device(): return (summed + b_dec[None, :]).astype(BF16)]
    unnamed x2 -> x1, local copies, waits for them, and re-layouts: 0.01 us -> 1.38 us
where the time goes in v2:
time: 51.9 us; the launch traced here: 51.7 us
  Pallas kernels  50.3 us (97%)
  local copies, waits for them, and re-layouts  1.38 us (3%)
    pallas_call x1, Pallas kernels, per_device(): pl.pallas_call(kernel, out_shape=jax.ShapeDtypeStruct((64, 256), BF16), i...  50.3 us
    unnamed x1, local copies, waits for them, and re-layouts  1.38 us

profile of v2, /device:TPU:7, one launch (start us, length us, event | category | flops | bytes accessed | tf_op | source)
XLA Modules:
  0.0 51.7 jit_solution(14526072647223810230)
XLA Ops:
  0.0 50.3 %shard_map.64 = bf16[64,256]{1,0:T(8,128)(2,1)} custom-call(s32[2,8,32]{2,1,0:T(8,128)} %slots_ref.1, bf16[2,512,128]{2,1,0:T(8,128)(2,1)} %x_hbm.1, bf16[2,128,2048]{2,1,0:T(8,128)(2,1)} %we_hbm.1, f32[2,2048]{1,0:T(2,128)} %be_hbm.1, bf16[2,16,128,256]{3,2,1,0:T(8,128)(2,1)} %bitcast.2, f32[1,256]{1,0:T(1,128)} %bitcast.3), custom_call_target="tpu_custom_call" | custom-call | flops 402653184 | bytes 4194304 | tf_op jit(solution)/shard_map/pallas_call | solution.py:238
  50.3 1.4 %copy.8 = bf16[64,256]{1,0:T(8,128)(2,1)} copy(bf16[64,256]{1,0:T(8,128)(2,1)} %shard_map.64) | data formatting | bytes 65536

commit v3 on v2

--- a/solution.py
+++ b/solution.py
@@ -11,6 +11,7 @@
 CHUNKS = 2
 F32 = jnp.float32
 BF16 = jnp.bfloat16
+FAR_FIRST = (10, 6, 9, 11, 14, 2, 5, 7, 8, 13, 15, 1, 3, 4, 12)
 
 
 def device(x, y, zh, c, t):
@@ -29,9 +30,8 @@
     zh = lax.rem(layer // 2, 2)
     y = lax.rem(layer // 4, 4)
     x = layer // 16
-    p = x * 4 + y
-    half = lax.rem(x, 2)
-    pair = x // 2
+    half = x // 2
+    pair = lax.rem(x, 2)
     crossed = lax.rem(half + c, 2)
     partner = device(x, y, zh, 1 - c, t)
     opposite = device(x, y, 1 - zh, c, t)
@@ -44,13 +44,8 @@
     def signal(dev):
         pl.semaphore_signal(barrier, inc=1, device_id=dev, device_id_type=MESH)
 
-    def greet_same(d, carry):
-        px, py = plane(d)
-        signal(device(px, py, zh, c, t))
-        return carry
-
     def greet_other(d, carry):
-        px, py = c + 2 * (d // 4), lax.rem(d, 4)
+        px, py = 2 * c + d // 4, lax.rem(d, 4)
 
         @pl.when((px != x) | (py != y))
         def _():
@@ -59,10 +54,12 @@
         return carry
 
     def greet_line(d, carry):
-        signal(device(x, y, zh, lax.rem(t, 2), lax.rem(t + d, 8)))
+        signal(device(x, y, zh, t // 4, lax.rem(t + d, 8)))
         return carry
 
-    lax.fori_loop(1, 16, greet_same, 0)
+    for d in FAR_FIRST:
+        px, py = plane(d)
+        signal(device(px, py, zh, c, t))
     lax.fori_loop(0, 8, greet_other, 0)
     signal(partner)
     lax.fori_loop(1, 8, greet_line, 0)
@@ -98,37 +95,51 @@
             w = jnp.concatenate([we[source, block_id(source, b, s)[0]] for s in range(4)], axis=1)
             target[b] = jnp.dot(xv[source, pl.ds(b * 64, 64), :], w, preferred_element_type=F32)
 
-    pl.semaphore_wait(barrier, 15 + 15 * crossed + 1 + 6 + 2 * lax.rem(t + c, 2) + zh)
+    pl.semaphore_wait(barrier, 15 + 15 * crossed + 1 + 6 + 2 * lax.rem(t // 4 + c, 2) + zh)
 
     @pl.when(zh == 1)
     def _():
         pl.semaphore_signal(zh_ready, inc=1, device_id=opposite, device_id_type=MESH)
 
     gives = []
-    for k in range(CHUNKS):
-        for i in range(4):
-            n = 4 * k + lax.rem(x + i, 4)
-            gives.append(remote(give.at[n], take.at[n], give_send.at[k, i], give_recv.at[k, i], partner))
+    order = []
+    for m in range(4):
+        for i in range(2):
+            side = half if i == 0 else 1 - half
+            n = m + side * (7 - 2 * m)
+            order.append((m, i, side, n))
+            gives.append(
+                remote(give.at[n], take.at[n], give_send.at[m, i], give_recv.at[m, i], partner)
+            )
             gives[-1].start()
-    for k in range(CHUNKS):
-        for i in range(4):
-            px = lax.rem(x + i, 4)
-            n = 4 * k + px
-            gives[4 * k + i].wait_recv()
-            pbuf[n] = (keep[n] + take[n]).astype(BF16)
-
-            def send_part(j, carry, k=k, i=i, px=px, n=n):
-                py = lax.rem(y + j, 4)
-                remote(
-                    pbuf.at[n, pl.ds(pl.multiple_of(py * 16, 16), 16)], rs_land.at[k, 4 * i + j - 1],
-                    rs_send.at[k], rs_recv.at[k], device(px, py, zh, c, t),
-                ).start()
-                return carry
-
-            lax.fori_loop(1 if i == 0 else 0, 4, send_part, 0)
+    def send_block(m, i, side, n, copy):
+        k, px = m // 2, 2 * side + m % 2
+        dx = lax.rem(px - x + 4, 4)
+        copy.wait_recv()
+        pbuf[n] = (keep[n] + take[n]).astype(BF16)
+
+        def send_part(j, carry, k=k, px=px, dx=dx, n=n):
+            py = lax.rem(y + j, 4)
+            remote(
+                pbuf.at[n, pl.ds(pl.multiple_of(py * 16, 16), 16)], rs_land.at[k, 4 * dx + j - 1],
+                rs_send.at[k], rs_recv.at[k], device(px, py, zh, c, t),
+            ).start()
+            return carry
+
+        lax.fori_loop(1, 4, send_part, 0)
+        if i == 0:
+
+            @pl.when(px != x)
+            def _(send_part=send_part):
+                send_part(0, 0)
+        else:
+            send_part(0, 0)
+
+    first = 4
+    for o, copy in zip(order[:first], gives[:first]):
+        send_block(*o, copy)
 
     swap_d = remote(wd_hbm, wd.at[1], wd_send, wd_recv, partner)
-    swap_d.start()
 
     @pl.when(zh == 0)
     def _():
@@ -138,16 +149,23 @@
     sums = []
     for k in range(CHUNKS):
         pltpu.make_async_copy(rs_land.at[k], rs_land.at[k], rs_recv.at[k]).wait()
-        total = pbuf[4 * k + x, rows, :].astype(F32)
+        m = 2 * k + pair
+        total = pbuf[m + half * (7 - 2 * m), rows, :].astype(F32)
         for d in range(15):
             total = total + rs_land[k, d].astype(F32)
         sums.append(total)
         zh_send[k] = total.astype(BF16)
         remote(zh_send.at[k], zh_land.at[k], zh_ss.at[k], zh_rs.at[k], opposite).start()
+        if k == 0:
+            for o, copy in zip(order[first:], gives[first:]):
+                send_block(*o, copy)
+
+    swap_d.start()
 
     pltpu.make_async_copy(be, be, local_sem.at[2]).wait()
     for k in range(CHUNKS):
-        b = 4 * k + x
+        m = 2 * k + pair
+        b = m + half * (7 - 2 * m)
         biases, masks = [], []
         for s in range(4):
             i, live = block_id(c, b, s)
@@ -161,12 +179,9 @@
         fown[k] = (jnp.maximum(pre, 0.0) * mask).astype(BF16)
         mine = feat.at[k, pair, c, rows]
 
-        def send_features(d, carry, k=k, mine=mine):
+        for d in FAR_FIRST:
             px, py = plane(d)
             remote(fown.at[k], mine, ag_send.at[k], ag_recv.at[k, pair], device(px, py, zh, half, t)).start()
-            return carry
-
-        lax.fori_loop(1, 16, send_features, 0)
 
         @pl.when(c == half)
         def _(k=k, mine=mine):
@@ -181,7 +196,7 @@
     for k in range(CHUNKS):
         for j in range(2):
             m = 2 * k + j
-            b = 2 * m + c
+            b = m + c * (7 - 2 * m)
             pltpu.make_async_copy(feat.at[k, j], feat.at[k, j], ag_recv.at[k, j]).wait()
             ids = [[block_id(s, b, i)[0] for i in range(4)] for s in range(2)]
             f = jnp.concatenate([feat[k, j, 0], feat[k, j, 1]], axis=1)
@@ -224,7 +239,7 @@
             remote(fown.at[k], fown.at[k], own_send.at[k], ag_recv.at[k, pair], partner).wait_send()
 
     for m in range(4):
-        b = 2 * m + c
+        b = m + c * (7 - 2 * m)
 
         @pl.when(b != t)
         def _(m=m):
@@ -237,7 +252,7 @@
     dma = pltpu.SemaphoreType.DMA
     return pl.pallas_call(
         kernel,
-        out_shape=jax.ShapeDtypeStruct((64, 256), BF16),
+        out_shape=pltpu.VMEM((64, 256), BF16),
         in_specs=[pl.BlockSpec(memory_space=pltpu.SMEM)]
         + [pl.BlockSpec(memory_space=pl.ANY)] * 4
         + [pl.BlockSpec(memory_space=pltpu.VMEM)],
@@ -259,8 +274,8 @@
             pltpu.VMEM((4, 2, 64, 256), BF16),
             pltpu.VMEM((8, 64, 256), BF16),
             dma((4,)),
-            dma((CHUNKS, 4)),
-            dma((CHUNKS, 4)),
+            dma((4, 2)),
+            dma((4, 2)),
             dma,
             dma,
             dma((CHUNKS,)),

time: 51.9 us -> 49.4 us (0.952)
  the two profiles are of different devices: /device:TPU:7 before, /device:TPU:97 now
where the time goes in v3:
time: 49.4 us; the launch traced here: 49.3 us
  Pallas kernels  48.6 us (98%)
  local copies, waits for them, and re-layouts  0.62 us (1%)
    pallas_call x1, Pallas kernels, per_device(): pl.pallas_call(kernel, out_shape=pltpu.VMEM((64, 256), BF16), in_specs=[p...  48.6 us

profile of v3, /device:TPU:97, one launch (start us, length us, event | category | flops | bytes accessed | tf_op | source)
XLA Modules:
  0.0 49.3 jit_solution(11785437889045855317)
XLA Ops:
  0.0 48.6 %shard_map.64 = bf16[64,256]{1,0:T(8,128)(2,1)S(1)} custom-call(s32[2,8,32]{2,1,0:T(8,128)} %slots_ref.1, bf16[2,512,128]{2,1,0:T(8,128)(2,1)} %x_hbm.1, bf16[2,128,2048]{2,1,0:T(8,128)(2,1)} %we_hbm.1, f32[2,2048]{1,0:T(2,128)} %be_hbm.1, bf16[2,16,128,256]{3,2,1,0:T(8,128)(2,1)} %bitcast.2, f32[1,256]{1,0:T(1,128)} %bitcast.3), custom_call_target="tpu_custom_call" | custom-call | flops 402653184 | bytes 4194304 | tf_op jit(solution)/shard_map/pallas_call | solution.py:253
  48.6 0.6 %copy.8 = bf16[64,256]{1,0:T(8,128)(2,1)} copy(bf16[64,256]{1,0:T(8,128)(2,1)S(1)} %shard_map.64) | data formatting | bytes 65536

commit v4 on v3

--- a/solution.py
+++ b/solution.py
@@ -21,7 +21,7 @@
 def kernel(
     slots_ref, x_hbm, we_hbm, be_hbm, wd_hbm, bd_ref, out_ref,
     xv, we, be, wd, keep, give, take, pbuf, rs_land, zh_send, zh_land, fown, feat, zbuf, zland,
-    local_sem, give_send, give_recv, wd_send, wd_recv, rs_send, rs_recv, zh_ready, zh_ss, zh_rs,
+    local_sem, give_send, give_recv, wd_send, wd_recv, rs_send, rs_recv, zh_ready, line_ready, zh_ss, zh_rs,
     ag_send, own_send, ag_recv, zl_send, zl_recv,
 ):
     layer = lax.axis_index("layer")
@@ -35,6 +35,9 @@
     crossed = lax.rem(half + c, 2)
     partner = device(x, y, zh, 1 - c, t)
     opposite = device(x, y, 1 - zh, c, t)
+    across = lax.rem(t + 4, 8)
+    relay = device(x, y, zh, c, across)
+    u = t + c * (7 - 2 * t)
 
     def plane(d):
         return lax.rem(x + d // 4, 4), lax.rem(y + lax.rem(d, 4), 4)
@@ -53,8 +56,11 @@
 
         return carry
 
-    def greet_line(d, carry):
-        signal(device(x, y, zh, t // 4, lax.rem(t + d, 8)))
+    def greet_line(pt, carry):
+        @pl.when((pt != t) & (pt - t <= 4) & (t - pt <= 4))
+        def _():
+            signal(device(x, y, zh, t // 4, pt))
+
         return carry
 
     for d in FAR_FIRST:
@@ -62,11 +68,16 @@
         signal(device(px, py, zh, c, t))
     lax.fori_loop(0, 8, greet_other, 0)
     signal(partner)
-    lax.fori_loop(1, 8, greet_line, 0)
+    lax.fori_loop(0, 8, greet_line, 0)
+
+    @pl.when(t // 4 != c)
+    def _():
+        signal(relay)
+
 
     @pl.when(zh == 0)
     def _():
-        signal(opposite)
+        signal(device(x, y, 1, c, across))
 
     load_x = pltpu.make_async_copy(x_hbm, xv, local_sem.at[0])
     load_d = pltpu.make_async_copy(wd_hbm, wd.at[0], local_sem.at[3])
@@ -95,11 +106,16 @@
             w = jnp.concatenate([we[source, block_id(source, b, s)[0]] for s in range(4)], axis=1)
             target[b] = jnp.dot(xv[source, pl.ds(b * 64, 64), :], w, preferred_element_type=F32)
 
-    pl.semaphore_wait(barrier, 15 + 15 * crossed + 1 + 6 + 2 * lax.rem(t // 4 + c, 2) + zh)
+    line = (u // 4) * (16 - 2 * u) + (1 - u // 4) * 7
+    pl.semaphore_wait(barrier, 15 + 15 * crossed + 1 + line + zh)
 
     @pl.when(zh == 1)
     def _():
-        pl.semaphore_signal(zh_ready, inc=1, device_id=opposite, device_id_type=MESH)
+        pl.semaphore_signal(
+            zh_ready, inc=1, device_id=device(x, y, 0, c, across), device_id_type=MESH
+        )
+
+    pl.semaphore_signal(line_ready, inc=1, device_id=relay, device_id_type=MESH)
 
     gives = []
     order = []
@@ -145,6 +161,8 @@
     def _():
         pl.semaphore_wait(zh_ready, 1)
 
+    pl.semaphore_wait(line_ready, 1)
+
     rows = pl.ds(pl.multiple_of(y * 16, 16), 16)
     sums = []
     for k in range(CHUNKS):
@@ -201,7 +219,7 @@
             ids = [[block_id(s, b, i)[0] for i in range(4)] for s in range(2)]
             f = jnp.concatenate([feat[k, j, 0], feat[k, j, 1]], axis=1)
 
-            for side in range(2):
+            for side in (1, 0):
                 w = jnp.concatenate([wd[side, s, ids[s][i]] for s in range(2) for i in range(4)], axis=0)
                 zbuf[m, side] = jnp.dot(f, w, preferred_element_type=F32).astype(BF16)
                 core = c if side == 0 else 1 - c
@@ -281,6 +299,7 @@
             dma((CHUNKS,)),
             dma((CHUNKS,)),
             pltpu.SemaphoreType.REGULAR,
+            pltpu.SemaphoreType.REGULAR,
             dma((CHUNKS,)),
             dma((CHUNKS,)),
             dma((CHUNKS,)),

time: 49.4 us -> 49.7 us (level)
  the two profiles are of different devices: /device:TPU:97 before, /device:TPU:64 now
where the time goes in v4:
time: 49.7 us; the launch traced here: 49.5 us
  Pallas kernels  48.9 us (98%)
  local copies, waits for them, and re-layouts  0.62 us (1%)
    pallas_call x1, Pallas kernels, per_device(): pl.pallas_call(kernel, out_shape=pltpu.VMEM((64, 256), BF16), in_specs=[p...  48.9 us

profile of v4, /device:TPU:64, one launch (start us, length us, event | category | flops | bytes accessed | tf_op | source)
XLA Modules:
  0.0 49.5 jit_solution(15444223984942869251)
XLA Ops:
  0.0 48.9 %shard_map.64 = bf16[64,256]{1,0:T(8,128)(2,1)S(1)} custom-call(s32[2,8,32]{2,1,0:T(8,128)} %slots_ref.1, bf16[2,512,128]{2,1,0:T(8,128)(2,1)} %x_hbm.1, bf16[2,128,2048]{2,1,0:T(8,128)(2,1)} %we_hbm.1, f32[2,2048]{1,0:T(2,128)} %be_hbm.1, bf16[2,16,128,256]{3,2,1,0:T(8,128)(2,1)} %bitcast.2, f32[1,256]{1,0:T(1,128)} %bitcast.3), custom_call_target="tpu_custom_call" | custom-call | flops 402653184 | bytes 4194304 | tf_op jit(solution)/shard_map/pallas_call | solution.py:271
  48.9 0.6 %copy.8 = bf16[64,256]{1,0:T(8,128)(2,1)} copy(bf16[64,256]{1,0:T(8,128)(2,1)S(1)} %shard_map.64) | data formatting | bytes 65536
